TPU v7x, 32 devices: a whole 2x2x4 slice. The times are simulated.
32 devices in a mesh: fsdp: 4 (over y, x), ctx: 4 (over z), tp: 2 (over core).
Axes of the slice: x: 2, y: 2, z: 4, core: 2. Of those that a mesh axis runs over, the one named last changes fastest.
Arguments:
- tokens: bfloat16 [12288, 896], P(('fsdp', 'ctx')), may hold values from -6 to 6
- cotangent: bfloat16 [12288, 896], P(('fsdp', 'ctx')), may hold values from -6 to 6
- seq_lengths: int32 [4, 3], P('fsdp'), may hold values from 1024 to 1024, as said below
- attn_gain: bfloat16 [896], P('fsdp'), may hold values from 0.5 to 1.5
- qkv_weight: bfloat16 [896, 1152], P('fsdp', 'tp'), may hold values from -0.1875 to 0.1875
- joined_bias: bfloat16 [2, 576], P('tp', 'fsdp'), may hold values from -0.3125 to 0.3125
- out_weight: bfloat16 [896, 896], P('tp', 'fsdp'), may hold values from -6 to 6
- mlp_gain: bfloat16 [896], P('fsdp'), may hold values from 0.5 to 1.5
- gate_up_weight: bfloat16 [896, 2, 4864], P('fsdp', None, 'tp'), may hold values from -0.1875 to 0.1875
- down_weight: bfloat16 [4864, 896], P('tp', 'fsdp'), may hold values from -0.078125 to 0.078125
Outputs:
- layer_out: bfloat16 [12288, 896], P(('fsdp', 'ctx'))
- token_grad: bfloat16 [12288, 896], P(('fsdp', 'ctx'))
- attn_gain_grad: float32 [896], P('fsdp')
- qkv_weight_grad: float32 [896, 1152], P('fsdp', 'tp')
- qkv_bias_grad: float32 [2, 576], P('tp', 'fsdp')
- out_weight_grad: float32 [896, 896], P('tp', 'fsdp')
- mlp_gain_grad: float32 [896], P('fsdp')
- gate_up_grad: float32 [896, 2, 4864], P('fsdp', None, 'tp')
- down_grad: float32 [4864, 896], P('tp', 'fsdp')
Inputs may be any that keep to these rules, and one draw needn't show every extreme that they name: `seq_lengths`: each row holds 3 lengths, each a multiple of 4, summing to 3072; in some row all lengths but the last are 1024.
All inputs are finite; a program needn't handle non-finite values.
Results may differ from a plain program's by a relative error of at most 0.024.
Values may be sent and summed in bfloat16 or wider, within the bound.
A program may use at most 128 MiB of HBM per device.

v0:
```python
import math

import jax
import jax.numpy as jnp
from jax import lax
from jax.sharding import PartitionSpec as P

HEAD_SIZE = 64


EPSILON = 1e-06
SCORE_SCALE = 0.125
THETA = 1000000.0
MASKED = -1e30


def places(row_ids, block_ids, pieces):
    seq_count = pieces.shape[0]
    seq_ends = jnp.cumsum(pieces, dtype=jnp.int32)
    starts = seq_ends - pieces
    sequence_index = jnp.sum(
        (row_ids[:, None] >= seq_ends[None, : seq_count - 1]).astype(jnp.int32),
        axis=1,
        dtype=jnp.int32,
    )
    chosen = sequence_index[:, None] == jnp.arange(seq_count, dtype=jnp.int32)[None, :]
    own_piece = jnp.sum(jnp.where(chosen, pieces[None, :], 0), axis=1, dtype=jnp.int32)
    first_row = jnp.sum(jnp.where(chosen, starts[None, :], 0), axis=1, dtype=jnp.int32)
    return (sequence_index, block_ids * own_piece + row_ids - first_row)


def turning(token_position, head_width):
    half_width = head_width // 2
    frequency = jnp.exp(
        jnp.arange(half_width, dtype=jnp.float32) * (-2.0 * math.log(THETA) / head_width)
    )
    angles = token_position.astype(jnp.float32)[:, None] * frequency[None, :]
    cosine_half = jnp.cos(angles)
    sine_half = jnp.sin(angles)
    return (
        jnp.concatenate([cosine_half, cosine_half], axis=-1),
        jnp.concatenate([sine_half, sine_half], axis=-1),
    )


def rotate(vectors, cosine_table, sine_table):
    half_width = vectors.shape[-1] // 2
    turned = jnp.concatenate([-vectors[..., half_width:], vectors[..., :half_width]], axis=-1)
    return vectors * cosine_table + turned * sine_table


def unrotate(gradient, cosine_table, sine_table):
    half_width = gradient.shape[-1] // 2
    weighted = gradient * sine_table
    turned = jnp.concatenate([weighted[..., half_width:], -weighted[..., :half_width]], axis=-1)
    return gradient * cosine_table + turned


def norm_forward(vectors, gain_row):
    inverse = lax.rsqrt(jnp.mean(vectors * vectors, axis=-1, keepdims=True) + EPSILON)
    unit_rows = vectors * inverse
    return (unit_rows, inverse, unit_rows * gain_row)


def norm_backward(upstream, unit_rows, inverse, gain_row):
    scaled = upstream * gain_row
    back = inverse * (scaled - unit_rows * jnp.mean(scaled * unit_rows, axis=-1, keepdims=True))
    return (back, jnp.sum(upstream * unit_rows, axis=0))


def body(
    tokens,
    cotangent,
    seq_lengths,
    attn_gain,
    qkv_weight,
    joined_bias,
    out_weight,
    mlp_gain,
    gate_up_weight,
    down_weight,
):
    gathered = (
        lax.all_gather(attn_gain, "fsdp", axis=0, tiled=True),
        lax.all_gather(qkv_weight, "fsdp", axis=0, tiled=True),
        lax.all_gather(joined_bias, "fsdp", axis=1, tiled=True),
        lax.all_gather(out_weight, "fsdp", axis=1, tiled=True),
        lax.all_gather(mlp_gain, "fsdp", axis=0, tiled=True),
        lax.all_gather(gate_up_weight, "fsdp", axis=0, tiled=True),
        lax.all_gather(down_weight, "fsdp", axis=1, tiled=True),
    )
    gain_one, wide_qkv, bias_row, wide_out, gain_two, wide_gate_up, wide_down = gathered
    count_of_rows = tokens.shape[0]
    slot_count = wide_qkv.shape[1] // HEAD_SIZE
    heads_per_group = slot_count - 2
    ctx_size = lax.axis_size("ctx")
    pieces = seq_lengths[0] // ctx_size
    local_rows = jnp.arange(count_of_rows, dtype=jnp.int32)
    query_seq, query_pos = places(local_rows, lax.axis_index("ctx"), pieces)
    cosine_table, sine_table = turning(query_pos, HEAD_SIZE)
    inputs = tokens.astype(jnp.float32)
    unit_one, inv_one, scaled_one = norm_forward(inputs, gain_one.astype(jnp.float32))
    normed_one = scaled_one.astype(jnp.bfloat16)
    projected_rows = jnp.dot(
        normed_one, wide_qkv, preferred_element_type=jnp.float32
    ) + bias_row.astype(jnp.float32)
    projected_rows = projected_rows.reshape(count_of_rows, slot_count, HEAD_SIZE)
    query_rows = rotate(
        projected_rows[:, :heads_per_group], cosine_table[:, None], sine_table[:, None]
    ).astype(jnp.bfloat16)
    keys_own = rotate(projected_rows[:, heads_per_group], cosine_table, sine_table).astype(
        jnp.bfloat16
    )
    values_own = projected_rows[:, heads_per_group + 1].astype(jnp.bfloat16)
    pairs = lax.all_gather(
        jnp.concatenate([keys_own, values_own], axis=-1), "ctx", axis=0, tiled=True
    )
    group_rows = pairs.shape[0]
    key_ids = jnp.arange(group_rows, dtype=jnp.int32)
    key_seq, key_pos = places(key_ids % count_of_rows, key_ids // count_of_rows, pieces)
    key_width = min(512, group_rows)
    block_count = group_rows // key_width

    def scores_at(block_no):
        row_start = block_no * key_width
        pair_rows = lax.dynamic_slice_in_dim(pairs, row_start, key_width, 0)
        seq_part = lax.dynamic_slice_in_dim(key_seq, row_start, key_width, 0)
        pos_part = lax.dynamic_slice_in_dim(key_pos, row_start, key_width, 0)
        allowed = (query_seq[:, None] == seq_part[None, :]) & (
            pos_part[None, :] <= query_pos[:, None]
        )
        key_part = pair_rows[:, :HEAD_SIZE]
        scores = (
            jnp.einsum("qhd,kd->hqk", query_rows, key_part, preferred_element_type=jnp.float32)
            * SCORE_SCALE
        )
        return (scores, allowed[None], key_part, pair_rows[:, HEAD_SIZE:])

    def peak_step(block_no, running):
        run_peak, run_total = running
        scores, allowed, key_part, value_part = scores_at(block_no)
        scores = jnp.where(allowed, scores, MASKED)
        new_peak = jnp.maximum(run_peak, jnp.max(scores, axis=-1))
        run_total = run_total * jnp.exp(run_peak - new_peak) + jnp.sum(
            jnp.where(allowed, jnp.exp(scores - new_peak[..., None]), 0.0), axis=-1
        )
        return (new_peak, run_total)

    start_peak = jnp.full((heads_per_group, count_of_rows), MASKED, jnp.float32)
    run_peak, run_total = lax.fori_loop(
        0, block_count, peak_step, (start_peak, jnp.zeros_like(start_peak))
    )
    log_total = run_peak + jnp.log(run_total)

    def soft_at(scores, allowed):
        return jnp.where(allowed, jnp.exp(scores - log_total[..., None]), 0.0)

    def output_step(block_no, running):
        scores, allowed, key_part, value_part = scores_at(block_no)
        soft_low = soft_at(scores, allowed).astype(jnp.bfloat16)
        return running + jnp.einsum(
            "hqk,kd->qhd", soft_low, value_part, preferred_element_type=jnp.float32
        )

    attended = lax.fori_loop(
        0,
        block_count,
        output_step,
        jnp.zeros((count_of_rows, heads_per_group, HEAD_SIZE), jnp.float32),
    )
    mixed_output = attended.reshape(count_of_rows, heads_per_group * HEAD_SIZE).astype(jnp.bfloat16)
    attn_out = lax.psum(
        jnp.dot(mixed_output, wide_out, preferred_element_type=jnp.float32).astype(jnp.bfloat16),
        "tp",
    ).astype(jnp.float32)
    hidden = inputs + attn_out
    unit_two, inv_two, scaled_two = norm_forward(hidden, gain_two.astype(jnp.float32))
    normed_two = scaled_two.astype(jnp.bfloat16)
    gate_up = jnp.einsum(
        "td,dcf->tcf", normed_two, wide_gate_up, preferred_element_type=jnp.float32
    )
    gate_in = gate_up[:, 0]
    up_in = gate_up[:, 1]
    sigmoid_gate = jax.nn.sigmoid(gate_in)
    activated = (gate_in * sigmoid_gate * up_in).astype(jnp.bfloat16)
    mlp_out = lax.psum(
        jnp.dot(activated, wide_down, preferred_element_type=jnp.float32).astype(jnp.bfloat16), "tp"
    ).astype(jnp.float32)
    layer_out = (hidden + mlp_out).astype(jnp.bfloat16)
    regathered = (
        lax.all_gather(attn_gain, "fsdp", axis=0, tiled=True),
        lax.all_gather(qkv_weight, "fsdp", axis=0, tiled=True),
        lax.all_gather(joined_bias, "fsdp", axis=1, tiled=True),
        lax.all_gather(out_weight, "fsdp", axis=1, tiled=True),
        lax.all_gather(mlp_gain, "fsdp", axis=0, tiled=True),
        lax.all_gather(gate_up_weight, "fsdp", axis=0, tiled=True),
        lax.all_gather(down_weight, "fsdp", axis=1, tiled=True),
    )
    gain_one, wide_qkv, bias_row, wide_out, gain_two, wide_gate_up, wide_down = regathered
    grad_top = cotangent.astype(jnp.float32)
    down_grad = jnp.einsum("tf,td->fd", activated, cotangent, preferred_element_type=jnp.float32)
    act_grad = jnp.einsum("td,fd->tf", cotangent, wide_down, preferred_element_type=jnp.float32)
    gate_grad = act_grad * up_in * sigmoid_gate * (1.0 + gate_in * (1.0 - sigmoid_gate))
    up_grad = act_grad * gate_in * sigmoid_gate
    gate_up_back = jnp.stack([gate_grad, up_grad], axis=1).astype(jnp.bfloat16)
    gate_up_grad = jnp.einsum(
        "td,tcf->dcf", normed_two, gate_up_back, preferred_element_type=jnp.float32
    )
    normed_two_grad = lax.psum(
        jnp.einsum(
            "tcf,dcf->td", gate_up_back, wide_gate_up, preferred_element_type=jnp.float32
        ).astype(jnp.bfloat16),
        "tp",
    ).astype(jnp.float32)
    hidden_norm_grad, mlp_gain_grad = norm_backward(
        normed_two_grad, unit_two, inv_two, gain_two.astype(jnp.float32)
    )
    hidden_grad = grad_top + hidden_norm_grad
    attn_back = hidden_grad.astype(jnp.bfloat16)
    out_weight_grad = jnp.einsum(
        "te,td->ed", mixed_output, attn_back, preferred_element_type=jnp.float32
    )
    mixed_grad = jnp.einsum("td,ed->te", attn_back, wide_out, preferred_element_type=jnp.float32)
    mixed_back = mixed_grad.astype(jnp.bfloat16).reshape(count_of_rows, heads_per_group, HEAD_SIZE)
    correction = jnp.einsum("qhd,qhd->hq", mixed_back.astype(jnp.float32), attended)

    def grad_step(block_no, running):
        query_grad, pair_grads = running
        scores, allowed, key_part, value_part = scores_at(block_no)
        soft_part = soft_at(scores, allowed)
        prob_grad = jnp.einsum(
            "qhd,kd->hqk", mixed_back, value_part, preferred_element_type=jnp.float32
        )
        score_grad = (soft_part * (prob_grad - correction[..., None])).astype(jnp.bfloat16)
        query_grad = query_grad + jnp.einsum(
            "hqk,kd->qhd", score_grad, key_part, preferred_element_type=jnp.float32
        )
        key_grad = jnp.einsum(
            "hqk,qhd->kd", score_grad, query_rows, preferred_element_type=jnp.float32
        )
        value_grad = jnp.einsum(
            "hqk,qhd->kd",
            soft_part.astype(jnp.bfloat16),
            mixed_back,
            preferred_element_type=jnp.float32,
        )
        pair_grads = lax.dynamic_update_slice_in_dim(
            pair_grads, jnp.concatenate([key_grad, value_grad], axis=-1), block_no * key_width, 0
        )
        return (query_grad, pair_grads)

    start_grads = (
        jnp.zeros((count_of_rows, heads_per_group, HEAD_SIZE), jnp.float32),
        jnp.zeros((group_rows, 2 * HEAD_SIZE), jnp.float32),
    )
    query_grad, pair_grads = lax.fori_loop(0, block_count, grad_step, start_grads)
    pair_own = lax.psum_scatter(
        pair_grads.astype(jnp.bfloat16), "ctx", scatter_dimension=0, tiled=True
    ).astype(jnp.float32)
    query_pre = unrotate(query_grad * SCORE_SCALE, cosine_table[:, None], sine_table[:, None])
    key_pre = unrotate(pair_own[:, :HEAD_SIZE] * SCORE_SCALE, cosine_table, sine_table)
    projected_back = jnp.concatenate(
        [query_pre, key_pre[:, None], pair_own[:, None, HEAD_SIZE:]], axis=1
    )
    projected_back = projected_back.reshape(count_of_rows, slot_count * HEAD_SIZE).astype(
        jnp.bfloat16
    )
    qkv_bias_grad = jnp.sum(projected_back, axis=0, dtype=jnp.float32)[None, :]
    qkv_weight_grad = jnp.einsum(
        "td,tc->dc", normed_one, projected_back, preferred_element_type=jnp.float32
    )
    normed_one_grad = lax.psum(
        jnp.einsum(
            "tc,dc->td", projected_back, wide_qkv, preferred_element_type=jnp.float32
        ).astype(jnp.bfloat16),
        "tp",
    ).astype(jnp.float32)
    input_norm_grad, attn_gain_grad = norm_backward(
        normed_one_grad, unit_one, inv_one, gain_one.astype(jnp.float32)
    )
    token_grad = (hidden_grad + input_norm_grad).astype(jnp.bfloat16)
    share_a, share_b, share_c, share_d, share_e, share_f, share_g = (
        lax.psum_scatter(
            attn_gain_grad.astype(jnp.bfloat16), "fsdp", scatter_dimension=0, tiled=True
        ).astype(jnp.float32),
        lax.psum_scatter(
            qkv_weight_grad.astype(jnp.bfloat16), "fsdp", scatter_dimension=0, tiled=True
        ).astype(jnp.float32),
        lax.psum_scatter(
            qkv_bias_grad.astype(jnp.bfloat16), "fsdp", scatter_dimension=1, tiled=True
        ).astype(jnp.float32),
        lax.psum_scatter(
            out_weight_grad.astype(jnp.bfloat16), "fsdp", scatter_dimension=1, tiled=True
        ).astype(jnp.float32),
        lax.psum_scatter(
            mlp_gain_grad.astype(jnp.bfloat16), "fsdp", scatter_dimension=0, tiled=True
        ).astype(jnp.float32),
        lax.psum_scatter(
            gate_up_grad.astype(jnp.bfloat16), "fsdp", scatter_dimension=0, tiled=True
        ).astype(jnp.float32),
        lax.psum_scatter(
            down_grad.astype(jnp.bfloat16), "fsdp", scatter_dimension=1, tiled=True
        ).astype(jnp.float32),
    )
    total_a, total_b, total_c, total_d, total_e, total_f, total_g = (
        lax.psum(share_a.astype(jnp.bfloat16), "ctx").astype(jnp.float32),
        lax.psum(share_b.astype(jnp.bfloat16), "ctx").astype(jnp.float32),
        lax.psum(share_c.astype(jnp.bfloat16), "ctx").astype(jnp.float32),
        lax.psum(share_d.astype(jnp.bfloat16), "ctx").astype(jnp.float32),
        lax.psum(share_e.astype(jnp.bfloat16), "ctx").astype(jnp.float32),
        lax.psum(share_f.astype(jnp.bfloat16), "ctx").astype(jnp.float32),
        lax.psum(share_g.astype(jnp.bfloat16), "ctx").astype(jnp.float32),
    )
    return (layer_out, token_grad, total_a, total_b, total_c, total_d, total_e, total_f, total_g)


def solution(mesh):
    placed = (
        P(("fsdp", "ctx"), None),
        P(("fsdp", "ctx"), None),
        P("fsdp", None),
        P("fsdp"),
        P("fsdp", "tp"),
        P("tp", "fsdp"),
        P("tp", "fsdp"),
        P("fsdp"),
        P("fsdp", None, "tp"),
        P("tp", "fsdp"),
    )
    return jax.shard_map(
        body,
        mesh=mesh,
        in_specs=placed,
        out_specs=(
            P(("fsdp", "ctx"), None),
            P(("fsdp", "ctx"), None),
            P("fsdp"),
            P("fsdp", "tp"),
            P("tp", "fsdp"),
            P("tp", "fsdp"),
            P("fsdp"),
            P("fsdp", None, "tp"),
            P("tp", "fsdp"),
        ),
        check_vma=False,
    )
```

profile of v0, /device:TPU:0, one launch (start us, length us, event | category | flops | bytes accessed | tf_op | source)
XLA Modules:
  0.0 985.6 jit_solution(14545223176211757317)
XLA Ops:
  15.0 11.5 %all-reduce.9 = (bf16[576]{0:T(1024)(128)(2,1)S(1)}, bf16[896]{0:T(1024)(128)(2,1)S(1)}, bf16[896]{0:T(1024)(128)(2,1)S(1)}) all-reduce(bf16[576]{0:T(1024)(128)(2,1)S(1)} %dynamic-update-slice.1, bf16[896]{0:T(1024)(128)(2,1)S(1)} %dynamic-update-slice, ...), channel_id=1, replica_groups=mesh['fsdp'=4,'ctx'=4,'tp'=2] {'fsdp'}, use_global_device_ids=true, to_apply=%add.1 | all-reduce | flops 2368 | bytes 9472
  28.2 13.4 %all_gather.31 = bf16[896,576]{1,0:T(8,128)(2,1)S(1)} all-gather(bf16[224,576]{1,0:T(8,128)(2,1)} %param.20), channel_id=1, replica_groups=mesh['fsdp'=4,'ctx'=4,'tp'=2] {'fsdp'}, dimensions={0}, use_global_device_ids=true | all-gather | bytes 1290240 | tf_op jit(solution)/shard_map/all_gather | solution.py:85
  49.0 18.8 %all_gather.33 = bf16[3072,128]{0,1:T(8,128)(2,1)} all-gather(bf16[768,128]{0,1:T(8,128)(2,1)S(1)} %pad_maximum_fusion.7), channel_id=1, replica_groups=mesh['fsdp'=4,'ctx'=4,'tp'=2] {'ctx'}, dimensions={0}, use_global_device_ids=true | all-gather | bytes 983040 | tf_op jit(solution)/shard_map/all_gather | solution.py:115
  69.7 85.7 %while.46 = (s32[]{:T(128)}, f32[7,768]{1,0:T(8,128)S(1)}, f32[7,768]{1,0:T(8,128)S(1)}, s32[768]{0:T(1024)S(1)}, s32[3072]{0:T(1024)S(1)}, /*index=5*/s32[3072]...) while((s32[]{:T(128)}, f32[7,768]{1,0:T(8,128)S(1)}, ...), condition=%wide.region_11.12_spmd.clone, body=%wide.region_8.11_spmd.clone.sunk | while | flops 375548160 | bytes 24251584 | solution.py:150
  70.2 6.9 fusion.139
  77.1 6.8 select_reduce_fusion.6
  84.5 6.9 fusion.139
  91.4 6.8 select_reduce_fusion.6
  98.8 6.9 fusion.139
  105.7 6.8 select_reduce_fusion.6
  113.1 6.9 fusion.139
  120.0 6.8 select_reduce_fusion.6
  127.4 6.9 fusion.139
  134.3 6.8 select_reduce_fusion.6
  141.6 6.9 fusion.139
  148.5 6.8 select_reduce_fusion.6
  155.4 36.7 %while.47 = (s32[]{:T(128)}, f32[768,7,64]{0,2,1:T(8,128)}, bf16[3072,128]{0,1:T(8,128)(2,1)}, s32[768]{0:T(1024)S(1)}, s32[3072]{0:T(1024)S(1)}, /*index=5*/s32...) while((s32[]{:T(128)}, f32[768,7,64]{0,2,1:T(8,128)}, ...), condition=%wide.region_13.14_spmd.clone, body=%wide.region_12.13_spmd.clone.sunk | while | flops 717520896 | bytes 4400336 | solution.py:165
  156.0 5.1 fusion.143
  161.6 5.7 fusion.143
  167.8 5.7 fusion.143
  174.0 5.7 fusion.143
  180.2 5.7 fusion.143
  186.4 5.7 fusion.143
  194.5 11.0 %all_gather.34 = bf16[448,896]{0,1:T(8,128)(2,1)S(1)} all-gather(bf16[448,224]{0,1:T(8,128)(2,1)S(1)} %copy.38), channel_id=1, replica_groups=mesh['fsdp'=4,'ctx'=4,'tp'=2] {'fsdp'}, dimensions={1}, use_global_device_ids=true | all-gather | bytes 1003520 | tf_op jit(solution)/shard_map/all_gather | solution.py:87
  213.5 14.8 %all-reduce.16.cloned.1.call-done = bf16[768,896]{1,0:T(8,128)(2,1)} async-done(((bf16[768,896]{1,0:T(8,128)(2,1)}), bf16[768,896]{1,0:T(8,128)(2,1)}) %all-reduce.16.cloned.1.call-update) | async-done | bytes 1376272 | tf_op jit(solution)/shard_map/psum | solution.py:172
  230.3 71.3 %all-gather.3.cloned.1.call-done = bf16[896,2,2432]{2,0,1:T(8,128)(2,1)} async-done(((bf16[224,2,2432]{2,0,1:T(8,128)(2,1)}), bf16[896,2,2432]{2,0,1:T(8,128)(2,1)}) %all-gather.3.cloned.1.call-update) | async-done | bytes 8716304 | tf_op jit(solution)/shard_map/all_gather | solution.py:89
  301.6 14.4 %fusion.88 = f32[768,2,2432]{2,0,1:T(8,128)} fusion(bf16[896,2,2432]{2,0,1:T(8,128)(2,1)} %all-gather.3.cloned.1.call-done, bf16[768,896]{1,0:T(8,128)(2,1)S(1)} %copy-done.3, bf16[768,896]{1,0:T(8,128)(2,1)S(1)} %copy-done.2, f32[896]{0:T(1024)S(1)} %convert_element_type.205, f32[768]{0:T(1024)S(1)} %add_rsqrt_fusion), kind=kOutput, calls=%fused_computation.174 | convolution fusion | flops 6698237952 | bytes 26417664 | tf_op jit(solution)/shard_map/td,dcf->tcf/dot_general | solution.py:179
  316.0 41.4 %all-gather.5.cloned.1.call-done = bf16[2432,896]{0,1:T(8,128)(2,1)} async-done(((bf16[2432,224]{0,1:T(8,128)(2,1)}), bf16[2432,896]{0,1:T(8,128)(2,1)}) %all-gather.5.cloned.1.call-update) | async-done | bytes 4358160 | tf_op jit(solution)/shard_map/all_gather | solution.py:90
  357.4 13.6 %fusion.45 = (bf16[768,1,2432]{2,0,1:T(8,128)(2,1)S(1)}, bf16[768,1,2432]{2,0,1:T(8,128)(2,1)}, bf16[768,2432]{1,0:T(8,128)(2,1)}) fusion(f32[768,2,2432]{2,0,1:T(8,128)} %fusion.88, bf16[768,896]{1,0:T(8,128)(2,1)} %param.17, bf16[2432,896]{0,1:T(8,128)(2,1)} %all-gather.5.cloned.1.call-done), kind=kOutput, calls=%fused_computation.65 | convolution fusion | flops 3376939008 | bytes 31883264 | tf_op jit(solution)/shard_map/td,fd->tf/dot_general | solution.py:202
  372.8 10.5 %bitcast_convert_fusion = bf16[768,896]{1,0:T(8,128)(2,1)} fusion(bf16[896,2,2432]{2,0,1:T(8,128)(2,1)S(1)} %copy-done.34, bf16[768,1,2432]{2,0,1:T(8,128)(2,1)} %get-tuple-element.759, bf16[768,1,2432]{2,0,1:T(8,128)(2,1)S(1)} %get-tuple-element.758), kind=kOutput, calls=%fused_computation.83 | convolution fusion | flops 6698532864 | bytes 17563648 | tf_op jit(solution)/shard_map/tcf,dcf->td/dot_general | solution.py:210
  383.6 20.0 %all-reduce.18.cloned.1.call-done = bf16[768,896]{1,0:T(8,128)(2,1)} async-done(((bf16[768,896]{1,0:T(8,128)(2,1)}), bf16[768,896]{1,0:T(8,128)(2,1)}) %all-reduce.18.cloned.1.call-update) | async-done | bytes 1376272 | tf_op jit(solution)/shard_map/psum | solution.py:209
  410.8 150.4 %while.48 = (s32[]{:T(128)}, f32[768,7,64]{0,2,1:T(8,128)S(1)}, bf16[3072,128]{0,1:T(8,128)(2,1)}, bf16[3072,128]{0,1:T(8,128)(2,1)}, s32[768]{0:T(1024)S(1)}, /...) while((s32[]{:T(128)}, f32[768,7,64]{0,2,1:T(8,128)S(1)}, ...), condition=%wide.region_20.21_spmd.clone, body=%wide.region_19.20_spmd.clone.sunk | while | flops 1791262720 | bytes 127288688 | solution.py:256
  412.1 6.6 fusion.151
  418.7 8.1 fusion.152
  432.1 3.8 fusion.153
  437.2 6.6 fusion.151
  443.8 8.1 fusion.152
  457.2 3.8 fusion.153
  462.2 6.6 fusion.151
  468.9 8.1 fusion.152
  482.3 3.8 fusion.153
  487.3 6.6 fusion.151
  494.0 8.1 fusion.152
  507.3 3.8 fusion.153
  512.4 6.6 fusion.151
  519.0 8.1 fusion.152
  532.4 3.8 fusion.153
  537.5 6.6 fusion.151
  544.1 8.1 fusion.152
  557.5 3.8 fusion.153
  561.6 4.7 convolution_convert_fusion.6
  569.9 16.1 %reduce-scatter.9.cloned.1.call-done = bf16[768,128]{0,1:T(8,128)(2,1)} async-done(((bf16[3072,128]{0,1:T(8,128)(2,1)}), bf16[768,128]{0,1:T(8,128)(2,1)}) %reduce-scatter.9.cloned.1.call-update) | async-done | bytes 196624 | tf_op jit(solution)/shard_map/reduce_scatter | solution.py:257
  591.7 7.9 convolution_convert_fusion.1
  601.0 13.6 %convolution_convert_fusion = bf16[896,2,2432]{2,0,1:T(8,128)(2,1)} fusion(bf16[768,1,2432]{2,0,1:T(8,128)(2,1)} %get-tuple-element.759, bf16[768,1,2432]{2,0,1:T(8,128)(2,1)} %copy-done.35, bf16[768,896]{1,0:T(8,128)(2,1)S(1)} %copy-done.5, bf16[768,896]{1,0:T(8,128)(2,1)S(1)} %copy-done.2, f32[896]{0:T(1024)S(1)} %convert_element_type.205, ...), kind=kOutput, calls=%fused_computation.54 | convolution fusion | flops 6717538304 | bytes 18946560 | tf_op jit(solution)/shard_map/td,tcf->dcf/dot_general | solution.py:206
  614.9 8.8 convolution_convert_fusion.3
  628.0 18.6 %reduce-scatter.11.cloned.1.call-done = bf16[224,576]{1,0:T(8,128)(2,1)} async-done(((bf16[896,576]{1,0:T(8,128)(2,1)}), bf16[224,576]{1,0:T(8,128)(2,1)}) %reduce-scatter.11.cloned.1.call-update) | async-done | bytes 258064 | tf_op jit(solution)/shard_map/reduce_scatter | solution.py:286
  646.6 57.6 %reduce-scatter.15.cloned.1.call-done = bf16[2432,224]{0,1:T(8,128)(2,1)} async-done(((bf16[2432,896]{0,1:T(8,128)(2,1)}), bf16[2432,224]{0,1:T(8,128)(2,1)}) %reduce-scatter.15.cloned.1.call-update) | async-done | bytes 1089552 | tf_op jit(solution)/shard_map/reduce_scatter | solution.py:301
  704.2 92.3 %reduce-scatter.13.cloned.1.call-done = bf16[224,2,2432]{2,0,1:T(8,128)(2,1)} async-done(((bf16[896,2,2432]{2,0,1:T(8,128)(2,1)}), bf16[224,2,2432]{2,0,1:T(8,128)(2,1)}) %reduce-scatter.13.cloned.1.call-update) | async-done | bytes 2179088 | tf_op jit(solution)/shard_map/reduce_scatter | solution.py:298
  797.8 24.0 %all-reduce.22.cloned.1.call-done = (bf16[768,896]{1,0:T(8,128)(2,1)}, bf16[768,896]{1,0:T(8,128)(2,1)}) async-done(((bf16[768,896]{1,0:T(8,128)(2,1)}, bf16[768,896]{1,0:T(8,128)(2,1)}), (bf16[768,896]{1,0:T(8,128)(2,1)}, bf16[768,896]{1,0:T(8,128)(2,1)})) %all-reduce.22.cloned.1.call-update) | async-done | bytes 2752528 | tf_op jit(solution)/shard_map/psum | solution.py:186
  824.3 10.2 %all-reduce.8 = (bf16[896]{0:T(1024)(128)(2,1)S(1)}, bf16[1,576]{1,0:T(2,128)(2,1)S(1)}, bf16[896]{0:T(1024)(128)(2,1)S(1)}) all-reduce(bf16[896]{0:T(1024)(128)(2,1)S(1)} %get-tuple-element.669, bf16[1,576]{1,0:T(2,128)(2,1)S(1)} %convert_element_type.227, ...), channel_id=3, replica_groups=mesh['fsdp'=4,'ctx'=4,'tp'=2] {'fsdp'}, use_global_device_ids=true, to_apply=%region_25.26.clone | all-reduce | flops 2368 | bytes 9472
  834.8 12.0 %all-reduce.6 = (bf16[224]{0:T(256)(128)(2,1)S(1)}, bf16[1,144]{1,0:T(2,128)(2,1)S(1)}, bf16[224]{0:T(256)(128)(2,1)S(1)}) all-reduce(bf16[224]{0:T(256)(128)(2,1)S(1)} %dynamic-slice.4, bf16[1,144]{1,0:T(2,128)(2,1)S(1)} %constant_dynamic-slice_fusion, ...), channel_id=1, replica_groups=mesh['fsdp'=4,'ctx'=4,'tp'=2] {'ctx'}, use_global_device_ids=true, to_apply=%region_26.27 | all-reduce | flops 592 | bytes 2368 | tf_op jit(solution)/shard_map/psum | solution.py:306
  848.5 5.1 fusion.51
  853.6 116.0 %all-reduce.20.cloned.1.call-done = (bf16[224,2,2432]{2,0,1:T(8,128)(2,1)}, bf16[224,576]{1,0:T(8,128)(2,1)}, bf16[448,224]{1,0:T(8,128)(2,1)}, bf16[2432,224]{0,1:T(8,128)(2,1)}) async-done(((bf16[224,2,2432]{2,0,1:T(8,128)(2,1)}, bf16[224,576]{1,0:T(8,128)(2,1)}, bf16[448,224]{1,0:T(8,128)(2,1)}, bf16[2432,224]{0,1:T(8,128)(2,1)}), (bf16[224,2,2432]{2,0,1:T(8,128)(2,1)}, bf16[224,576]{1,0:T(8,128)(2,1)}, ...) | async-done | bytes 3727376 | tf_op jit(solution)/shard_map/psum | solution.py:311
  969.6 5.5 copy.41
  (299 shorter events, 107.0 us)
Async XLA Ops:
  8.0 33.5 %copy-start.2 = (bf16[768,896]{1,0:T(8,128)(2,1)S(1)}, bf16[768,896]{1,0:T(8,128)(2,1)}, u32[]{:S(2)}) copy-start(bf16[768,896]{1,0:T(8,128)(2,1)} %param.16) | copy-start | bytes 4128772
  8.0 220.3 %all-reduce.16.cloned.1.call-start = ((), (), s32[]{:S(2)}) async-start(), calls=%async_computation.5 | async-start | bytes 2752512 | tf_op jit(solution)/shard_map/psum | solution.py:172
  26.5 16.4 %copy-start.30 = (f32[896]{0:T(1024)}, f32[896]{0:T(1024)S(1)}, u32[]{:S(2)}) copy-start(f32[896]{0:T(1024)S(1)} %convert_element_type.193) | copy-start | bytes 10756
  28.2 14.7 %copy-start.32 = (f32[768]{0:T(1024)}, f32[768]{0:T(1024)S(1)}, u32[]{:S(2)}) copy-start(f32[768]{0:T(1024)S(1)} %add_rsqrt_fusion.1) | copy-start | bytes 9220
  41.5 1.3 copy-start.14
  42.9 6.1 copy-start.7
  45.7 22.3 %copy-start.10 = (f32[768,7,32]{0,2,1:T(8,128)S(1)}, f32[768,7,32]{0,2,1:T(8,128)}, u32[]{:S(2)}) copy-start(f32[768,7,32]{0,2,1:T(8,128)} %get-tuple-element.763) | copy-start | bytes 2064388
  45.7 22.3 %copy-start.11 = (f32[768,7,32]{0,2,1:T(8,128)S(1)}, f32[768,7,32]{0,2,1:T(8,128)}, u32[]{:S(2)}) copy-start(f32[768,7,32]{0,2,1:T(8,128)} %get-tuple-element.764) | copy-start | bytes 2064388
  46.3 23.4 %copy-start.18 = (f32[768,32]{0,1:T(8,128)}, f32[768,32]{0,1:T(8,128)S(1)}, u32[]{:S(2)}) copy-start(f32[768,32]{0,1:T(8,128)S(1)} %get-tuple-element.778) | copy-start | bytes 294916
  46.3 23.4 %copy-start.22 = (f32[768,32]{0,1:T(8,128)}, f32[768,32]{0,1:T(8,128)S(1)}, u32[]{:S(2)}) copy-start(f32[768,32]{0,1:T(8,128)S(1)} %get-tuple-element.779) | copy-start | bytes 294916
  155.4 39.0 %copy-start.28 = (bf16[448,224]{1,0:T(8,128)(2,1)S(1)}, bf16[448,224]{1,0:T(8,128)(2,1)}, u32[]{:S(2)}) copy-start(bf16[448,224]{1,0:T(8,128)(2,1)} %param.22) | copy-start | bytes 602116
  205.5 6.8 copy-start.17
  209.1 92.5 %all-gather.3.cloned.1.call-start = ((), (), s32[]{:S(2)}) async-start(), calls=%async_computation.6 | async-start | bytes 10895360 | tf_op jit(solution)/shard_map/all_gather | solution.py:89
  212.4 145.0 %all-gather.5.cloned.1.call-start = ((), (), s32[]{:S(2)}) async-start(), calls=%async_computation.7 | async-start | bytes 5447680 | tf_op jit(solution)/shard_map/all_gather | solution.py:90
  213.0 190.6 %all-reduce.18.cloned.1.call-start = ((), (), s32[]{:S(2)}) async-start(), calls=%async_computation.8 | async-start | bytes 2752512 | tf_op jit(solution)/shard_map/psum | solution.py:209
  228.3 73.3 %copy-start.3 = (bf16[768,896]{1,0:T(8,128)(2,1)S(1)}, bf16[768,896]{1,0:T(8,128)(2,1)}, u32[]{:S(2)}) copy-start(bf16[768,896]{1,0:T(8,128)(2,1)} %all-reduce.16.cloned.1.call-done) | copy-start | bytes 4128772
  357.4 15.4 %copy-start.34 = (bf16[896,2,2432]{2,0,1:T(8,128)(2,1)S(1)}, bf16[896,2,2432]{2,0,1:T(8,128)(2,1)}, u32[]{:S(2)}) copy-start(bf16[896,2,2432]{2,0,1:T(8,128)(2,1)} %all-gather.3.cloned.1.call-done) | copy-start | bytes 26148868
  371.0 1.8 copy-start.35
  383.3 202.6 %reduce-scatter.9.cloned.1.call-start = ((), (), s32[]{:S(2)}) async-start(), calls=%async_computation.9 | async-start | bytes 983040 | tf_op jit(solution)/shard_map/reduce_scatter | solution.py:257
  403.6 3.1 copy-start.4
  403.6 3.1 copy-start.8
  403.6 3.1 copy-start.12
  406.7 3.0 copy-start.9
  418.7 10.4 %copy-start.1 = (f32[512,768,7]{1,0,2:T(8,128)S(1)}, f32[512,768,7]{1,0,2:T(8,128)}, u32[]{:S(2)}) copy-start(f32[512,768,7]{1,0,2:T(8,128)} %fusion.151) | copy-start | bytes 33030148 | tf_op jit(solution)/shard_map/while
  426.8 2.4 copy-start
  426.8 2.3 copy-start.6
  426.8 2.3 copy-start.26
  443.8 10.4 %copy-start.1 = (f32[512,768,7]{1,0,2:T(8,128)S(1)}, f32[512,768,7]{1,0,2:T(8,128)}, u32[]{:S(2)}) copy-start(f32[512,768,7]{1,0,2:T(8,128)} %fusion.151) | copy-start | bytes 33030148 | tf_op jit(solution)/shard_map/while
  451.9 2.4 copy-start
  451.9 2.3 copy-start.6
  451.9 2.3 copy-start.26
  468.9 10.4 %copy-start.1 = (f32[512,768,7]{1,0,2:T(8,128)S(1)}, f32[512,768,7]{1,0,2:T(8,128)}, u32[]{:S(2)}) copy-start(f32[512,768,7]{1,0,2:T(8,128)} %fusion.151) | copy-start | bytes 33030148 | tf_op jit(solution)/shard_map/while
  477.0 2.4 copy-start
  477.0 2.3 copy-start.6
  477.0 2.3 copy-start.26
  494.0 10.4 %copy-start.1 = (f32[512,768,7]{1,0,2:T(8,128)S(1)}, f32[512,768,7]{1,0,2:T(8,128)}, u32[]{:S(2)}) copy-start(f32[512,768,7]{1,0,2:T(8,128)} %fusion.151) | copy-start | bytes 33030148 | tf_op jit(solution)/shard_map/while
  502.0 2.4 copy-start
  502.1 2.3 copy-start.6
  502.1 2.3 copy-start.26
  519.0 10.4 %copy-start.1 = (f32[512,768,7]{1,0,2:T(8,128)S(1)}, f32[512,768,7]{1,0,2:T(8,128)}, u32[]{:S(2)}) copy-start(f32[512,768,7]{1,0,2:T(8,128)} %fusion.151) | copy-start | bytes 33030148 | tf_op jit(solution)/shard_map/while
  527.1 2.4 copy-start
  527.1 2.3 copy-start.6
  527.1 2.3 copy-start.26
  544.1 10.4 %copy-start.1 = (f32[512,768,7]{1,0,2:T(8,128)S(1)}, f32[512,768,7]{1,0,2:T(8,128)}, u32[]{:S(2)}) copy-start(f32[512,768,7]{1,0,2:T(8,128)} %fusion.151) | copy-start | bytes 33030148 | tf_op jit(solution)/shard_map/while
  552.2 2.4 copy-start
  552.2 2.3 copy-start.6
  552.2 2.3 copy-start.26
  561.3 65.0 %reduce-scatter.17.cloned.1.call-start = ((), (), s32[]{:S(2)}) async-start(), calls=%async_computation.13 | async-start | bytes 1146880
  566.2 2.4 copy-start.24
  568.6 78.0 %reduce-scatter.11.cloned.1.call-start = ((), (), s32[]{:S(2)}) async-start(), calls=%async_computation.10 | async-start | bytes 1433600 | tf_op jit(solution)/shard_map/reduce_scatter | solution.py:286
  568.9 19.0 %copy-start.19 = (f32[768,32]{0,1:T(8,128)S(1)}, f32[768,32]{0,1:T(8,128)}, u32[]{:S(2)}) copy-start(f32[768,32]{0,1:T(8,128)} %copy-done.18) | copy-start | bytes 294916
  569.9 19.2 %copy-start.31 = (f32[896]{0:T(1024)S(1)}, f32[896]{0:T(1024)}, u32[]{:S(2)}) copy-start(f32[896]{0:T(1024)} %copy-done.30) | copy-start | bytes 10756
  569.9 19.2 %copy-start.33 = (f32[768]{0:T(1024)S(1)}, f32[768]{0:T(1024)}, u32[]{:S(2)}) copy-start(f32[768]{0:T(1024)} %copy-done.32) | copy-start | bytes 9220
  589.1 2.6 copy-start.13
  591.6 112.5 %reduce-scatter.15.cloned.1.call-start = ((), (), s32[]{:S(2)}) async-start(), calls=%async_computation.12 | async-start | bytes 5447680 | tf_op jit(solution)/shard_map/reduce_scatter | solution.py:301
  599.6 1.4 copy-start.5
  599.6 196.8 %reduce-scatter.13.cloned.1.call-start = ((), (), s32[]{:S(2)}) async-start(), calls=%async_computation.11 | async-start | bytes 10895360 | tf_op jit(solution)/shard_map/reduce_scatter | solution.py:298
  614.6 207.3 %all-reduce.22.cloned.1.call-start = ((), (), s32[]{:S(2)}) async-start(), calls=%async_computation.15 | async-start | bytes 5505024 | tf_op jit(solution)/shard_map/psum | solution.py:186
  614.9 8.8 copy-start.15
  614.9 8.8 copy-start.21
  626.2 343.4 %all-reduce.20.cloned.1.call-start = ((), (), s32[]{:S(2)}) async-start(), calls=%async_computation.14 | async-start | bytes 7569408 | tf_op jit(solution)/shard_map/psum | solution.py:311
  969.6 5.5 copy-start.16
  975.1 1.5 copy-start.27
  975.1 2.3 copy-start.29
  (3 other events, 3.0 us)
Sparse Core Ops, SparseCore 0:
  209.2 19.0 all-reduce.15
  383.5 20.0 all-reduce.17
  561.4 24.4 reduce-scatter.8
  588.7 26.1 reduce-scatter.16
  618.2 28.3 reduce-scatter.10
  650.1 54.0 reduce-scatter.14
  707.3 89.0 reduce-scatter.12
  799.4 22.4 all-reduce.21
  825.3 144.3 all-reduce.19
Sparse Core Ops, SparseCore 1:
  212.4 89.1 all-gather.2
  303.4 53.9 all-gather.4
where the time goes:
time: 991 us; the launch traced here: 986 us
  waiting for transfers between devices  473 us (48%)
  matrix products  296 us (30%)
  other arithmetic  89.9 us (9%)
  blocking collectives  76.9 us (8%)
  local copies, waits for them, and re-layouts  29.1 us (3%)
  between operations  18.7 us (2%)
    psum x1, waiting for transfers between devices, body(): lax.psum(share_f.astype(jnp.bfloat16), 'ctx').astype(jnp.float32)  116 us
    reduce_scatter x1, waiting for transfers between devices, body(): lax.psum_scatter(gate_up_grad.astype(jnp.bfloat16), 'fsdp', scatter_dimen...  92.3 us
    dot_general x12, matrix products, scores_at(): jnp.einsum('qhd,kd->hqk', query_rows, key_part, preferred_element_type=jn...  81.2 us
    all_gather x1, waiting for transfers between devices, body(): lax.all_gather(gate_up_weight, 'fsdp', axis=0, tiled=True)  71.3 us
    reduce_scatter x1, waiting for transfers between devices, body(): lax.psum_scatter(down_grad.astype(jnp.bfloat16), 'fsdp', scatter_dimensio...  57.6 us
    dot_general x6, matrix products, grad_step(): jnp.einsum('qhd,kd->hqk', mixed_back, value_part, preferred_element_type=...  48.4 us
    all_gather x1, waiting for transfers between devices, body(): lax.all_gather(down_weight, 'fsdp', axis=1, tiled=True)  41.4 us
    reduce_sum x6, other arithmetic, peak_step(): jnp.sum(jnp.where(allowed, jnp.exp(scores - new_peak[..., None]), 0.0), a...  40.7 us
  transfers between devices with their start and end apart: 11, of which 10 were waited for; matrix products, arithmetic and copies ran while one was open for 8% of the time, Pallas kernels for 0%

commit v1 on v0

v1 whole, which is shorter than its diff:
```python
import math

import jax
import jax.numpy as jnp
from jax import lax
from jax.experimental import pallas as pl
from jax.experimental.pallas import tpu as pltpu
from jax.sharding import PartitionSpec as P

HEAD_SIZE = 64


EPSILON = 1e-06
SCORE_SCALE = 0.125
THETA = 1000000.0
MASKED = -1e30


def places(row_ids, block_ids, pieces):
    seq_count = pieces.shape[0]
    seq_ends = jnp.cumsum(pieces, dtype=jnp.int32)
    starts = seq_ends - pieces
    sequence_index = jnp.sum(
        (row_ids[:, None] >= seq_ends[None, : seq_count - 1]).astype(jnp.int32),
        axis=1,
        dtype=jnp.int32,
    )
    chosen = sequence_index[:, None] == jnp.arange(seq_count, dtype=jnp.int32)[None, :]
    own_piece = jnp.sum(jnp.where(chosen, pieces[None, :], 0), axis=1, dtype=jnp.int32)
    first_row = jnp.sum(jnp.where(chosen, starts[None, :], 0), axis=1, dtype=jnp.int32)
    return (sequence_index, block_ids * own_piece + row_ids - first_row)


def turning(token_position, head_width):
    half_width = head_width // 2
    frequency = jnp.exp(
        jnp.arange(half_width, dtype=jnp.float32) * (-2.0 * math.log(THETA) / head_width)
    )
    angles = token_position.astype(jnp.float32)[:, None] * frequency[None, :]
    cosine_half = jnp.cos(angles)
    sine_half = jnp.sin(angles)
    return (
        jnp.concatenate([cosine_half, cosine_half], axis=-1),
        jnp.concatenate([sine_half, sine_half], axis=-1),
    )


def rotate(vectors, cosine_table, sine_table):
    half_width = vectors.shape[-1] // 2
    turned = jnp.concatenate([-vectors[..., half_width:], vectors[..., :half_width]], axis=-1)
    return vectors * cosine_table + turned * sine_table


def unrotate(gradient, cosine_table, sine_table):
    half_width = gradient.shape[-1] // 2
    weighted = gradient * sine_table
    turned = jnp.concatenate([weighted[..., half_width:], -weighted[..., :half_width]], axis=-1)
    return gradient * cosine_table + turned


def norm_forward(vectors, gain_row):
    inverse = lax.rsqrt(jnp.mean(vectors * vectors, axis=-1, keepdims=True) + EPSILON)
    unit_rows = vectors * inverse
    return (unit_rows, inverse, unit_rows * gain_row)


def norm_backward(upstream, unit_rows, inverse, gain_row):
    scaled = upstream * gain_row
    back = inverse * (scaled - unit_rows * jnp.mean(scaled * unit_rows, axis=-1, keepdims=True))
    return (back, jnp.sum(upstream * unit_rows, axis=0))


MIN_SEQ = 1024
VMEM_LIMIT = 48 * 1024 * 1024


def nt_dot(left, right):
    return lax.dot_general(left, right, (((1,), (1,)), ((), ())), preferred_element_type=jnp.float32)


def nn_dot(left, right):
    return lax.dot_general(left, right, (((1,), (0,)), ((), ())), preferred_element_type=jnp.float32)


def load_pairs(pair_ref):
    chunks = pair_ref.shape[0]
    key_t = jnp.concatenate([pair_ref[j, :HEAD_SIZE, :] for j in range(chunks)], axis=1)
    value_t = jnp.concatenate([pair_ref[j, HEAD_SIZE:, :] for j in range(chunks)], axis=1)
    return key_t, value_t


def flip(block):
    return block.astype(jnp.float32).T.astype(jnp.bfloat16)


def causal_bias(me, keys, width):
    key_pos = lax.broadcasted_iota(jnp.int32, (keys, width), 0)
    query_pos = lax.broadcasted_iota(jnp.int32, (keys, width), 1) + me * width
    return jnp.where(key_pos <= query_pos, 0.0, MASKED)


def attend_kernel(me_ref, query_ref, pair_ref, out_ref, log_ref):
    width = query_ref.shape[1]
    heads = query_ref.shape[0] // HEAD_SIZE
    key_t, value_t = load_pairs(pair_ref)
    key = flip(key_t)
    bias = causal_bias(me_ref[0], key.shape[0], width)
    for h in range(heads):
        rows = slice(h * HEAD_SIZE, (h + 1) * HEAD_SIZE)
        scores = nn_dot(key, query_ref[rows, :]) + bias
        peak = jnp.max(scores, axis=0, keepdims=True)
        soft = jnp.exp(scores - peak)
        total = jnp.sum(soft, axis=0, keepdims=True)
        soft = (soft * (1.0 / total)).astype(jnp.bfloat16)
        out_ref[rows, :] = nn_dot(value_t, soft).astype(jnp.bfloat16)
        log_ref[h : h + 1, :] = peak + jnp.log(total)
    log_ref[heads:, :] = jnp.zeros_like(log_ref[heads:, :])


def attend_back_kernel(me_ref, query_ref, pair_ref, log_ref, grad_ref, query_grad_ref, pair_grad_ref):
    width = query_ref.shape[1]
    heads = query_ref.shape[0] // HEAD_SIZE
    key_t, value_t = load_pairs(pair_ref)
    key, value = flip(key_t), flip(value_t)
    bias = causal_bias(me_ref[0], key.shape[0], width)
    key_grad = jnp.zeros(key.shape, jnp.float32)
    value_grad = jnp.zeros(key.shape, jnp.float32)
    for h in range(heads):
        rows = slice(h * HEAD_SIZE, (h + 1) * HEAD_SIZE)
        query_t, grad_t = query_ref[rows, :], grad_ref[rows, :]
        soft = jnp.exp(nn_dot(key, query_t) + bias - log_ref[h : h + 1, :])
        prob_grad = nn_dot(value, grad_t)
        delta = jnp.sum(soft * prob_grad, axis=0, keepdims=True)
        score_grad = (soft * (prob_grad - delta)).astype(jnp.bfloat16)
        query_grad_ref[rows, :] = nn_dot(key_t, score_grad)
        key_grad = key_grad + nt_dot(score_grad, query_t)
        value_grad = value_grad + nt_dot(soft.astype(jnp.bfloat16), grad_t)
    both = jnp.concatenate([key_grad, value_grad], axis=1).astype(jnp.bfloat16)
    for j in range(pair_grad_ref.shape[0]):
        pair_grad_ref[j] = both[j * width : (j + 1) * width]


def even_attention(query_t, pairs_t, width):
    depth, rows = query_t.shape
    ctx = pairs_t.shape[0]
    me = lax.axis_index("ctx").astype(jnp.int32).reshape(1)
    scalar = pl.BlockSpec(memory_space=pltpu.SMEM)
    wide = pl.BlockSpec((depth, width), lambda s: (0, s))
    pair = pl.BlockSpec((ctx, 2 * HEAD_SIZE, width), lambda s: (0, 0, s))
    logs = pl.BlockSpec((8, width), lambda s: (0, s))
    params = pltpu.CompilerParams(vmem_limit_bytes=VMEM_LIMIT)
    mixed_t, log_total = pl.pallas_call(
        attend_kernel,
        grid=(rows // width,),
        in_specs=[scalar, wide, pair],
        out_specs=[wide, logs],
        out_shape=[
            jax.ShapeDtypeStruct((depth, rows), jnp.bfloat16),
            jax.ShapeDtypeStruct((8, rows), jnp.float32),
        ],
        compiler_params=params,
        name="attend",
    )(me, query_t, pairs_t)

    def back(mixed_back_t):
        return pl.pallas_call(
            attend_back_kernel,
            grid=(rows // width,),
            in_specs=[scalar, wide, pair, logs, wide],
            out_specs=[wide, pl.BlockSpec((ctx, width, 2 * HEAD_SIZE), lambda s: (0, s, 0))],
            out_shape=[
                jax.ShapeDtypeStruct((depth, rows), jnp.float32),
                jax.ShapeDtypeStruct((ctx, rows, 2 * HEAD_SIZE), jnp.bfloat16),
            ],
            compiler_params=params,
            name="attend_back",
        )(me, query_t, pairs_t, log_total, mixed_back_t)

    return mixed_t, back


def ragged_attention(query_t, pairs_t, query_seq, query_pos, pieces):
    ctx = pairs_t.shape[0]
    depth, count_of_rows = query_t.shape
    heads = depth // HEAD_SIZE
    query_rows = query_t.reshape(heads, HEAD_SIZE, count_of_rows).transpose(2, 0, 1)
    pairs = pairs_t.transpose(0, 2, 1).reshape(ctx * count_of_rows, 2 * HEAD_SIZE)
    group_rows = pairs.shape[0]
    key_ids = jnp.arange(group_rows, dtype=jnp.int32)
    key_seq, key_pos = places(key_ids % count_of_rows, key_ids // count_of_rows, pieces)
    key_width = min(512, group_rows)
    block_count = group_rows // key_width

    def scores_at(block_no):
        row_start = block_no * key_width
        pair_rows = lax.dynamic_slice_in_dim(pairs, row_start, key_width, 0)
        seq_part = lax.dynamic_slice_in_dim(key_seq, row_start, key_width, 0)
        pos_part = lax.dynamic_slice_in_dim(key_pos, row_start, key_width, 0)
        allowed = (query_seq[:, None] == seq_part[None, :]) & (
            pos_part[None, :] <= query_pos[:, None]
        )
        key_part = pair_rows[:, :HEAD_SIZE]
        scores = jnp.einsum(
            "qhd,kd->hqk", query_rows, key_part, preferred_element_type=jnp.float32
        )
        return (scores, allowed[None], key_part, pair_rows[:, HEAD_SIZE:])

    def peak_step(block_no, running):
        run_peak, run_total = running
        scores, allowed, key_part, value_part = scores_at(block_no)
        scores = jnp.where(allowed, scores, MASKED)
        new_peak = jnp.maximum(run_peak, jnp.max(scores, axis=-1))
        run_total = run_total * jnp.exp(run_peak - new_peak) + jnp.sum(
            jnp.where(allowed, jnp.exp(scores - new_peak[..., None]), 0.0), axis=-1
        )
        return (new_peak, run_total)

    start_peak = jnp.full((heads, count_of_rows), MASKED, jnp.float32)
    run_peak, run_total = lax.fori_loop(
        0, block_count, peak_step, (start_peak, jnp.zeros_like(start_peak))
    )
    log_total = run_peak + jnp.log(run_total)

    def soft_at(scores, allowed):
        return jnp.where(allowed, jnp.exp(scores - log_total[..., None]), 0.0)

    def output_step(block_no, running):
        scores, allowed, key_part, value_part = scores_at(block_no)
        soft_low = soft_at(scores, allowed).astype(jnp.bfloat16)
        return running + jnp.einsum(
            "hqk,kd->qhd", soft_low, value_part, preferred_element_type=jnp.float32
        )

    attended = lax.fori_loop(
        0, block_count, output_step, jnp.zeros((count_of_rows, heads, HEAD_SIZE), jnp.float32)
    )
    mixed_t = attended.transpose(1, 2, 0).reshape(depth, count_of_rows).astype(jnp.bfloat16)

    def back(mixed_back_t):
        mixed_back = mixed_back_t.reshape(heads, HEAD_SIZE, count_of_rows).transpose(2, 0, 1)
        correction = jnp.einsum("qhd,qhd->hq", mixed_back.astype(jnp.float32), attended)

        def grad_step(block_no, running):
            query_grad, pair_grads = running
            scores, allowed, key_part, value_part = scores_at(block_no)
            soft_part = soft_at(scores, allowed)
            prob_grad = jnp.einsum(
                "qhd,kd->hqk", mixed_back, value_part, preferred_element_type=jnp.float32
            )
            score_grad = (soft_part * (prob_grad - correction[..., None])).astype(jnp.bfloat16)
            query_grad = query_grad + jnp.einsum(
                "hqk,kd->qhd", score_grad, key_part, preferred_element_type=jnp.float32
            )
            key_grad = jnp.einsum(
                "hqk,qhd->kd", score_grad, query_rows, preferred_element_type=jnp.float32
            )
            value_grad = jnp.einsum(
                "hqk,qhd->kd",
                soft_part.astype(jnp.bfloat16),
                mixed_back,
                preferred_element_type=jnp.float32,
            )
            pair_grads = lax.dynamic_update_slice_in_dim(
                pair_grads,
                jnp.concatenate([key_grad, value_grad], axis=-1),
                block_no * key_width,
                0,
            )
            return (query_grad, pair_grads)

        start_grads = (
            jnp.zeros((count_of_rows, heads, HEAD_SIZE), jnp.float32),
            jnp.zeros((group_rows, 2 * HEAD_SIZE), jnp.float32),
        )
        query_grad, pair_grads = lax.fori_loop(0, block_count, grad_step, start_grads)
        query_grad_t = query_grad.transpose(1, 2, 0).reshape(depth, count_of_rows)
        return query_grad_t, pair_grads.astype(jnp.bfloat16).reshape(
            ctx, count_of_rows, 2 * HEAD_SIZE
        )

    return mixed_t, back


def dot32(spec, left, right):
    return jnp.einsum(spec, left, right, preferred_element_type=jnp.float32)


def pair_sum(partial):
    low = partial.astype(jnp.bfloat16)
    if lax.axis_size("tp") != 2:
        return lax.psum(low, "tp").astype(jnp.float32)
    other = lax.ppermute(low, "tp", [(0, 1), (1, 0)])
    return low.astype(jnp.float32) + other.astype(jnp.float32)


def pair_join(half):
    if lax.axis_size("tp") != 2:
        return lax.all_gather(half, "tp", axis=0, tiled=True)
    other = lax.ppermute(half, "tp", [(0, 1), (1, 0)])
    first = lax.axis_index("tp") == 0
    return jnp.concatenate([jnp.where(first, half, other), jnp.where(first, other, half)], axis=0)


def pair_half(rows):
    count = rows.shape[0] // lax.axis_size("tp")
    return lax.dynamic_slice_in_dim(rows, lax.axis_index("tp") * count, count, 0)


PLANE = ("fsdp", "tp")


def body(
    tokens,
    cotangent,
    seq_lengths,
    attn_gain,
    qkv_weight,
    joined_bias,
    out_weight,
    mlp_gain,
    gate_up_weight,
    down_weight,
):
    fsdp_size = lax.axis_size("fsdp")
    ctx_size = lax.axis_size("ctx")
    rows = tokens.shape[0]
    part, columns = qkv_weight.shape
    model = part * fsdp_size
    slots = columns // HEAD_SIZE
    heads = slots - 2
    depth = heads * HEAD_SIZE
    bias_part = joined_bias.shape[1]
    hidden_units = down_weight.shape[0]
    ff = hidden_units // fsdp_size

    small = jnp.concatenate(
        [
            jnp.pad(attn_gain[None], ((0, 0), (0, columns - part))),
            jnp.pad(mlp_gain[None], ((0, 0), (0, columns - part))),
            jnp.pad(joined_bias, ((0, 0), (0, columns - bias_part))),
            jnp.zeros((13, columns), jnp.bfloat16),
        ],
        axis=0,
    )
    packed = lax.all_gather(
        jnp.concatenate([qkv_weight, small], axis=0), "fsdp", axis=0, tiled=False
    )
    wide_qkv = packed[:, :part].reshape(model, columns)
    gain_one = packed[:, part, :part].reshape(model).astype(jnp.float32)
    gain_two = packed[:, part + 1, :part].reshape(model).astype(jnp.float32)
    bias_row = packed[:, part + 2, :bias_part].reshape(columns).astype(jnp.float32)

    pieces = seq_lengths[0] // ctx_size
    local_rows = jnp.arange(rows, dtype=jnp.int32)
    query_seq, query_pos = places(local_rows, lax.axis_index("ctx"), pieces)
    half = HEAD_SIZE // 2
    frequency = jnp.exp(
        jnp.arange(half, dtype=jnp.float32) * (-2.0 * math.log(THETA) / HEAD_SIZE)
    )
    angles = frequency[:, None] * query_pos.astype(jnp.float32)[None, :]
    cosine, sine = jnp.cos(angles)[None], jnp.sin(angles)[None]

    inputs = tokens.astype(jnp.float32)
    unit_one, inv_one, scaled_one = norm_forward(inputs, gain_one)
    normed_one = scaled_one.astype(jnp.bfloat16)
    projected = dot32("dc,td->ct", wide_qkv, normed_one) + bias_row[:, None]
    projected = projected.reshape(slots, HEAD_SIZE, rows)
    first, second = projected[: heads + 1, :half], projected[: heads + 1, half:]
    turned = jnp.concatenate(
        [first * cosine - second * sine, second * cosine + first * sine], axis=1
    ).astype(jnp.bfloat16)
    query_t = (turned[:heads] * SCORE_SCALE).reshape(depth, rows)
    pair_t = jnp.concatenate([turned[heads], projected[heads + 1].astype(jnp.bfloat16)], axis=0)
    pairs_t = lax.all_gather(pair_t, "ctx", axis=0, tiled=False)

    wide_out = lax.all_gather(out_weight, "fsdp", axis=1, tiled=True)
    gate_up_parts = gate_up_weight.reshape(part, 2, fsdp_size, ff).transpose(2, 0, 1, 3)
    gate_up_parts = lax.all_to_all(
        gate_up_parts.reshape(fsdp_size, part, 2 * ff), "fsdp", 0, 0, tiled=True
    )
    wide_gate_up = gate_up_parts.reshape(model, 2 * ff)
    down_parts = lax.all_to_all(
        down_weight.reshape(fsdp_size, ff, part), "fsdp", 0, 0, tiled=True
    )
    wide_down = down_parts.transpose(1, 0, 2).reshape(ff, model)
    cot_all = lax.all_gather(pair_half(cotangent), PLANE, axis=0, tiled=True)

    seqs = seq_lengths.shape[1]
    if rows * ctx_size == seqs * MIN_SEQ and (rows // seqs) % 128 == 0:
        mixed_t, attention_back = even_attention(query_t, pairs_t, rows // seqs)
    else:
        mixed_t, attention_back = ragged_attention(query_t, pairs_t, query_seq, query_pos, pieces)

    hidden = inputs + pair_sum(dot32("et,ed->td", mixed_t, wide_out))
    unit_two, inv_two, scaled_two = norm_forward(hidden, gain_two)
    normed_two = lax.all_gather(
        pair_half(scaled_two.astype(jnp.bfloat16)), PLANE, axis=0, tiled=True
    )
    gate_up = dot32("td,df->tf", normed_two, wide_gate_up)
    gate_in, up_in = gate_up[:, :ff], gate_up[:, ff:]
    sigmoid_gate = jax.nn.sigmoid(gate_in)
    activated = (gate_in * sigmoid_gate * up_in).astype(jnp.bfloat16)
    act_grad = dot32("td,fd->tf", cot_all, wide_down)
    gate_grad = act_grad * up_in * sigmoid_gate * (1.0 + gate_in * (1.0 - sigmoid_gate))
    up_grad = act_grad * gate_in * sigmoid_gate
    gate_up_back = jnp.concatenate([gate_grad, up_grad], axis=1).astype(jnp.bfloat16)
    normed_two_grad = lax.psum_scatter(
        dot32("tf,df->td", gate_up_back, wide_gate_up).astype(jnp.bfloat16),
        PLANE,
        scatter_dimension=0,
        tiled=True,
    )
    mlp_out = lax.psum_scatter(
        dot32("tf,fd->td", activated, wide_down).astype(jnp.bfloat16),
        PLANE,
        scatter_dimension=0,
        tiled=True,
    )
    layer_out = (hidden + pair_join(mlp_out).astype(jnp.float32)).astype(jnp.bfloat16)

    gate_up_grad = dot32("td,tf->df", normed_two, gate_up_back).astype(jnp.bfloat16)
    down_grad = dot32("tf,td->fd", activated, cot_all).astype(jnp.bfloat16)
    gate_up_grad = lax.psum_scatter(
        gate_up_grad.reshape(fsdp_size, part, 2 * ff), "ctx", scatter_dimension=1, tiled=True
    )
    gate_up_grad = lax.all_to_all(gate_up_grad, "fsdp", 0, 0, tiled=True)
    gate_up_grad = lax.all_gather(gate_up_grad, "ctx", axis=1, tiled=True)
    gate_up_total = (
        gate_up_grad.reshape(fsdp_size, part, 2, ff)
        .transpose(1, 2, 0, 3)
        .reshape(part, 2, hidden_units)
        .astype(jnp.float32)
    )
    down_grad = lax.psum_scatter(
        down_grad.reshape(ff, fsdp_size, part).transpose(1, 0, 2),
        "ctx",
        scatter_dimension=1,
        tiled=True,
    )
    down_grad = lax.all_to_all(down_grad, "fsdp", 0, 0, tiled=True)
    down_grad = lax.all_gather(down_grad, "ctx", axis=1, tiled=True)
    down_total = down_grad.reshape(hidden_units, part).astype(jnp.float32)

    hidden_norm_grad, mlp_gain_grad = norm_backward(
        pair_join(normed_two_grad).astype(jnp.float32), unit_two, inv_two, gain_two
    )
    hidden_grad = cotangent.astype(jnp.float32) + hidden_norm_grad
    attn_back = hidden_grad.astype(jnp.bfloat16)
    mixed_back_t = dot32("ed,td->et", wide_out, attn_back).astype(jnp.bfloat16)
    out_weight_grad = dot32("td,et->de", attn_back, mixed_t).astype(jnp.bfloat16)

    query_grad_t, pair_grads = attention_back(mixed_back_t)
    pair_own = lax.psum_scatter(pair_grads, "ctx", scatter_dimension=0, tiled=True)
    pair_own = pair_own.reshape(rows, 2 * HEAD_SIZE).astype(jnp.float32).T
    turned_grad = jnp.concatenate(
        [query_grad_t.reshape(heads, HEAD_SIZE, rows) * SCORE_SCALE, pair_own[None, :HEAD_SIZE]],
        axis=0,
    )
    first, second = turned_grad[:, :half], turned_grad[:, half:]
    turned_grad = jnp.concatenate(
        [first * cosine + second * sine, second * cosine - first * sine], axis=1
    )
    projected_back = (
        jnp.concatenate([turned_grad, pair_own[None, HEAD_SIZE:]], axis=0)
        .reshape(columns, rows)
        .astype(jnp.bfloat16)
    )
    normed_one_grad = pair_sum(dot32("ct,dc->td", projected_back, wide_qkv))
    input_norm_grad, attn_gain_grad = norm_backward(normed_one_grad, unit_one, inv_one, gain_one)
    token_grad = (hidden_grad + input_norm_grad).astype(jnp.bfloat16)

    qkv_bias_grad = jnp.sum(projected_back, axis=1, dtype=jnp.float32).astype(jnp.bfloat16)
    qkv_weight_grad = dot32("td,ct->dc", normed_one, projected_back).astype(jnp.bfloat16)
    wide_grads = jnp.concatenate([qkv_weight_grad, out_weight_grad], axis=1)
    wide_grads = wide_grads.reshape(fsdp_size, part, columns + depth)
    bias_back = qkv_bias_grad.reshape(fsdp_size, 1, bias_part)
    bias_back = jnp.pad(bias_back, ((0, 0), (0, 0), (0, columns + depth - bias_part)))
    bias_back = jnp.pad(bias_back, ((0, 0), (0, 15), (0, 0)))
    small_grads = jnp.concatenate([wide_grads, bias_back], axis=1)
    small_own = lax.psum_scatter(small_grads, "fsdp", scatter_dimension=0, tiled=True)[0]
    small_own = lax.psum(small_own, "ctx").astype(jnp.float32)
    gains = lax.psum(
        jnp.stack([attn_gain_grad, mlp_gain_grad], axis=0), ("fsdp", "ctx")
    )
    gains = lax.dynamic_slice_in_dim(gains, lax.axis_index("fsdp") * part, part, 1)
    return (
        layer_out,
        token_grad,
        gains[0],
        small_own[:part, :columns],
        small_own[part : part + 1, :bias_part],
        small_own[:part, columns:].T,
        gains[1],
        gate_up_total,
        down_total,
    )


def solution(mesh):
    placed = (
        P(("fsdp", "ctx"), None),
        P(("fsdp", "ctx"), None),
        P("fsdp", None),
        P("fsdp"),
        P("fsdp", "tp"),
        P("tp", "fsdp"),
        P("tp", "fsdp"),
        P("fsdp"),
        P("fsdp", None, "tp"),
        P("tp", "fsdp"),
    )
    return jax.shard_map(
        body,
        mesh=mesh,
        in_specs=placed,
        out_specs=(
            P(("fsdp", "ctx"), None),
            P(("fsdp", "ctx"), None),
            P("fsdp"),
            P("fsdp", "tp"),
            P("tp", "fsdp"),
            P("tp", "fsdp"),
            P("fsdp"),
            P("fsdp", None, "tp"),
            P("tp", "fsdp"),
        ),
        check_vma=False,
    )
```

time: 991 us -> 720 us (0.73)
  matrix products: 296 us -> 78.5 us
  waiting for transfers between devices: 473 us -> 336 us
  local copies, waits for them, and re-layouts: 29.1 us -> 102 us
  other arithmetic: 89.9 us -> 30.4 us
  Pallas kernels: 0 us -> 37.8 us
  blocking collectives: 76.9 us -> 94.7 us
  starting transfers between devices: 1.62 us -> 14.2 us
    dot_general x54 -> x12, matrix products: 296 us -> 78.5 us  [dot32(): return jnp.einsum(spec, left, right, preferred_element_type=jnp.float32)]
    psum x4 -> x0, waiting for transfers between devices: 175 us -> none  [the longest x1 116 us: body(): lax.psum(share_f.astype(jnp.bfloat16), 'ctx').astype(jnp.float32)]
    unnamed x12 -> x14, waiting for transfers between devices: 0.72 us -> 77 us
    reduce_scatter x4 -> x3, waiting for transfers between devices: 184 us -> 117 us  [the longest x1 59.2 us: body(): lax.psum_scatter(dot32('tf,fd->td', activated, wide_down).astype(jnp.bflo...]
    all_to_all x0 -> x3, waiting for transfers between devices: none -> 47.7 us  [the longest x1 35.8 us: body(): lax.all_to_all(gate_up_parts.reshape(fsdp_size, part, 2 * ff), 'fsdp', 0,...]
    reduce_sum x7 -> x1, other arithmetic: 40.9 us -> 1.09 us  [body(): jnp.sum(projected_back, axis=1, dtype=jnp.float32).astype(jnp.bfloat16)]
    pallas_call x0 -> x2, Pallas kernels: none -> 37.8 us  [the longest x1 20.6 us: back(): pl.pallas_call(attend_back_kernel, grid=(rows // width,), in_specs=[scala...]
    convert_element_type x2 -> x10, local copies, waits for them, and re-layouts: 0.74 us -> 30.9 us  [the longest x3 22.6 us: body(): gate_up_total = gate_up_grad.reshape(fsdp_size, part, 2, ff).transpose(1,...]
  transfers between devices with their start and end apart: 11 -> 18, of which waited for: 10 -> 13; matrix products, arithmetic and copies ran while one was open for 8% -> 21% of each run, Pallas kernels for 0% -> 0%
where the time goes in v1:
time: 720 us; the launch traced here: 710 us
  waiting for transfers between devices  336 us (47%)
  local copies, waits for them, and re-layouts  102 us (14%)
  blocking collectives  94.7 us (13%)
  matrix products  78.5 us (11%)
  Pallas kernels  37.8 us (5%)
  other arithmetic  30.4 us (4%)
  between operations  15.4 us (2%)
  starting transfers between devices  14.2 us (2%)
    dot_general x12, matrix products, dot32(): return jnp.einsum(spec, left, right, preferred_element_type=jnp.float32)  78.5 us
    unnamed x14, waiting for transfers between devices  77 us
    reduce_scatter x1, waiting for transfers between devices, body(): lax.psum_scatter(dot32('tf,fd->td', activated, wide_down).astype(jnp.bflo...  59.2 us
    reduce_scatter x1, waiting for transfers between devices, body(): lax.psum_scatter(dot32('tf,df->td', gate_up_back, wide_gate_up).astype(jn...  57.8 us
    all_gather x1, waiting for transfers between devices, body(): gate_up_grad = lax.all_gather(gate_up_grad, 'ctx', axis=1, tiled=True)  49.7 us
    psum x1, blocking collectives, body(): lax.psum(jnp.stack([attn_gain_grad, mlp_gain_grad], axis=0), ('fsdp', 'ct...  42.1 us
    all_to_all x1, waiting for transfers between devices, body(): lax.all_to_all(gate_up_parts.reshape(fsdp_size, part, 2 * ff), 'fsdp', 0,...  35.8 us
    unnamed x86, local copies, waits for them, and re-layouts  25.2 us
  transfers between devices with their start and end apart: 18, of which 13 were waited for; matrix products, arithmetic and copies ran while one was open for 21% of the time, Pallas kernels for 0%

profile of v1, /device:TPU:0, one launch (start us, length us, event | category | flops | bytes accessed | tf_op | source)
XLA Modules:
  0.0 709.7 jit_solution(7531042939963158495)
XLA Ops:
  7.3 1.2 copy.105
  12.7 16.9 %all_gather.31 = bf16[448,896]{0,1:T(8,128)(2,1)S(1)} all-gather(bf16[448,224]{0,1:T(8,128)(2,1)S(1)} %copy.109), channel_id=1, replica_groups=mesh['fsdp'=4,'ctx'=4,'tp'=2] {'fsdp'}, dimensions={1}, use_global_device_ids=true | all-gather | bytes 1003520 | tf_op jit(solution)/shard_map/all_gather | solution.py:376
  30.4 13.9 %all-gather.17.cloned.1.call-done = bf16[4,240,576]{1,2,0:T(8,128)(2,1)} async-done(((bf16[1,240,576]{1,2,0:T(8,128)(2,1)}), bf16[4,240,576]{1,2,0:T(8,128)(2,1)}) %all-gather.17.cloned.1.call-update) | async-done | bytes 1105936 | tf_op jit(solution)/shard_map/all_gather | solution.py:345
  44.3 1.4 convert_reduce_fusion
  45.8 2.4 copy.108
  49.4 2.6 convolution_add_fusion
  52.4 19.6 %all-gather.1 = bf16[512,768]{1,0:T(8,128)(2,1)S(1)} all-gather(bf16[128,768]{1,0:T(8,128)(2,1)S(1)} %pad_maximum_fusion.8), channel_id=3, replica_groups=mesh['fsdp'=4,'ctx'=4,'tp'=2] {'ctx'}, dimensions={0}, use_global_device_ids=true | all-gather | bytes 983040 | tf_op jit(solution)/shard_map/all_gather | solution.py:374
  72.0 17.2 %attend.1 = (bf16[448,768]{1,0:T(8,128)(2,1)S(1)}, f32[8,768]{1,0:T(8,128)S(1)}) custom-call(s32[1]{0:T(128)} %bitcast.me_ref, bf16[448,768]{1,0:T(8,128)(2,1)S(1)} %bitcast.87, bf16[4,128,768]{2,1,0:T(8,128)(2,1)S(1)} %bitcast.85), custom_call_target="tpu_custom_call" | custom-call | tf_op jit(solution)/shard_map/attend/pallas_call | solution.py:152
  89.2 2.1 convolution_convert_fusion.3
  91.4 3.4 collective-permute-done
  94.8 2.9 multiply_reduce_fusion
  97.7 2.3 broadcast_multiply_fusion
  100.0 1.5 copy-done.9
  104.0 7.5 %reshape.285 = bf16[224,2,4,608]{3,2,1,0:T(4,128)(2,1)} reshape(bf16[224,2,2432]{2,1,0:T(2,128)(2,1)} %param.18) | data formatting | bytes 4358144 | tf_op jit(solution)/shard_map/reshape | solution.py:377
  111.5 4.8 copy.132
  116.4 5.8 reshape.286
  122.1 4.7 all-to-all-start
  126.8 2.3 reshape.288
  130.3 35.8 %all-to-all-done = bf16[4,224,1216]{2,1,0:T(8,128)(2,1)} async-done(((bf16[4,224,1216]{2,1,0:T(8,128)(2,1)}), bf16[4,224,1216]{2,1,0:T(8,128)(2,1)}, u32[]{:S(2)}, u32[]{:S(2)}) %all-to-all-start) | async-done | bytes 2179104 | tf_op jit(solution)/shard_map/all_to_all | solution.py:378
  166.1 3.5 all-to-all-start.1
  169.7 13.8 %fusion.39 = f32[3072,1216]{0,1:T(8,128)} fusion(bf16[3072,896]{1,0:T(8,128)(2,1)} %all-gather.9.cloned.1.call-done, bf16[896,1216]{1,0:T(8,128)(2,1)} %bitcast.13), kind=kOutput, calls=%fused_computation.118 | convolution fusion | flops 6694109184 | bytes 22626304 | tf_op jit(solution)/shard_map/td,df->tf/dot_general | solution.py:285
  183.5 7.5 %all-to-all-done.1 = bf16[4,608,224]{1,2,0:T(8,128)(2,1)S(1)} async-done(((bf16[4,608,224]{1,2,0:T(8,128)(2,1)}), bf16[4,608,224]{1,2,0:T(8,128)(2,1)S(1)}, u32[]{:S(2)}, u32[]{:S(2)}) %all-to-all-start.1) | async-done | bytes 1089568 | tf_op jit(solution)/shard_map/all_to_all | solution.py:382
  191.0 25.1 %all-gather.11.cloned.1.call-done = bf16[3072,896]{1,0:T(8,128)(2,1)} async-done(((bf16[384,896]{1,0:T(8,128)(2,1)}), bf16[3072,896]{1,0:T(8,128)(2,1)}) %all-gather.11.cloned.1.call-update) | async-done | bytes 5505040 | tf_op jit(solution)/shard_map/all_gather | solution.py:386
  216.1 12.8 %multiply_convert_fusion.1 = (bf16[3072,608]{0,1:T(8,128)(2,1)S(1)}, bf16[3072,608]{0,1:T(8,128)(2,1)S(1)}, bf16[3072,608]{0,1:T(8,128)(2,1)}) fusion(f32[3072,1216]{0,1:T(8,128)} %fusion.39, bf16[3072,896]{1,0:T(8,128)(2,1)} %all-gather.11.cloned.1.call-done, bf16[608,896]{0,1:T(8,128)(2,1)S(1)} %bitcast.102), kind=kOutput, calls=%fused_computation.2 | convolution fusion | flops 3376939008 | bytes 32743424 | tf_op jit(solution)/shard_map/td,fd->tf/dot_general | solution.py:285
  228.9 1.9 copy-done.36
  231.9 11.7 %convolution_convert_fusion.1 = bf16[3072,896]{1,0:T(8,128)(2,1)} fusion(bf16[896,1216]{1,0:T(8,128)(2,1)} %bitcast.13, bf16[3072,608]{0,1:T(8,128)(2,1)S(1)} %get-tuple-element.95, bf16[3072,608]{0,1:T(8,128)(2,1)S(1)} %get-tuple-element.94), kind=kOutput, calls=%fused_computation.6 | convolution fusion | flops 6711803904 | bytes 15155200 | tf_op jit(solution)/shard_map/tf,df->td/dot_general | solution.py:285
  243.9 57.8 %reduce-scatter.12.cloned.1.call-done = bf16[384,896]{1,0:T(8,128)(2,1)} async-done(((bf16[3072,896]{1,0:T(8,128)(2,1)}), bf16[384,896]{1,0:T(8,128)(2,1)}) %reduce-scatter.12.cloned.1.call-update) | async-done | bytes 688144 | tf_op jit(solution)/shard_map/reduce_scatter | solution.py:407
  301.7 2.4 collective-permute-done.2
  304.0 1.2 broadcast_select_fusion.1
  305.3 1.2 fusion.12
  308.7 20.6 %attend_back.1 = (f32[448,768]{1,0:T(8,128)S(1)}, bf16[4,768,128]{2,1,0:T(8,128)(2,1)S(1)}) custom-call(s32[1]{0:T(128)} %bitcast.me_ref, bf16[448,768]{1,0:T(8,128)(2,1)S(1)} %bitcast.88, bf16[4,128,768]{2,1,0:T(8,128)(2,1)S(1)} %bitcast.86, f32[8,768]{1,0:T(8,128)S(1)} %copy-done.2, bf16[448,768]{1,0:T(8,128)(2,1)S(1)} %fusion.24.grad_ref), custom_call_target="tpu_custom_call" | custom-call | tf_op jit(solution)/shard_map/attend_back/pallas_call | solution.py:166
  330.6 13.2 %fusion.6 = bf16[896,1216]{0,1:T(8,128)(2,1)} fusion(bf16[3072,896]{1,0:T(8,128)(2,1)} %all-gather.9.cloned.1.call-done, bf16[3072,608]{0,1:T(8,128)(2,1)} %copy-done.37, bf16[3072,608]{0,1:T(8,128)(2,1)} %copy-done.36), kind=kOutput, calls=%fused_computation.17 | convolution fusion | flops 6710140928 | bytes 15155200 | tf_op jit(solution)/shard_map/td,tf->df/dot_general | solution.py:285
  343.7 4.1 copy.116
  347.9 4.9 copy.131
  352.8 4.7 reshape.307
  363.2 2.0 copy.112
  365.2 1.8 slice_bitcast_fusion.1
  367.0 1.7 copy.113
  368.7 1.3 multiply_add_fusion
  373.2 1.4 pad_maximum_fusion.5
  374.6 2.9 copy.114
  377.6 1.5 fusion.22
  379.3 8.9 %convolution_convert_fusion = bf16[3072,896]{1,0:T(8,128)(2,1)} fusion(bf16[3072,608]{0,1:T(8,128)(2,1)} %get-tuple-element.96, bf16[608,896]{0,1:T(8,128)(2,1)S(1)} %bitcast.103), kind=kOutput, calls=%fused_computation.5 | convolution fusion | flops 3349807104 | bytes 10330112 | tf_op jit(solution)/shard_map/tf,fd->td/dot_general | solution.py:285
  388.7 14.3 %reduce-scatter.16.cloned.1.call-done = bf16[56,4864]{1,0:T(8,128)(2,1)} async-done(((bf16[224,4864]{1,0:T(8,128)(2,1)}), bf16[56,4864]{1,0:T(8,128)(2,1)}) %reduce-scatter.16.cloned.1.call-update) | async-done | bytes 544784
  403.0 1.7 reshape.308
  404.8 16.1 %all_to_all.20 = bf16[4,56,1216]{2,1,0:T(8,128)(2,1)} all-to-all(bf16[4,56,1216]{2,1,0:T(8,128)(2,1)S(1)} %copy.126), channel_id=1, replica_groups=mesh['fsdp'=4,'ctx'=4,'tp'=2] {'fsdp'}, dimensions={0} | all-to-all | bytes 1089536 | tf_op jit(solution)/shard_map/all_to_all | solution.py:426
  421.0 8.0 %convolution_convert_fusion.4 = bf16[608,896]{1,0:T(8,128)(2,1)S(1)} fusion(bf16[3072,608]{0,1:T(8,128)(2,1)} %get-tuple-element.96, bf16[3072,896]{1,0:T(8,128)(2,1)} %all-gather.11.cloned.1.call-done), kind=kOutput, calls=%fused_computation.48 | convolution fusion | flops 3347599360 | bytes 10330112 | tf_op jit(solution)/shard_map/tf,td->fd/dot_general | solution.py:285
  430.1 2.1 copy.119
  432.3 8.6 %reduce-scatter.18.cloned.1.call-done = bf16[1,240,1024]{2,1,0:T(8,128)(2,1)} async-done(((bf16[4,240,1024]{2,1,0:T(8,128)(2,1)}), bf16[1,240,1024]{2,1,0:T(8,128)(2,1)}) %reduce-scatter.18.cloned.1.call-update) | async-done | bytes 491536
  440.9 2.5 convolution_convert_fusion.2
  443.4 59.2 %reduce-scatter.10.cloned.1.call-done = bf16[384,896]{1,0:T(8,128)(2,1)} async-done(((bf16[3072,896]{1,0:T(8,128)(2,1)}), bf16[384,896]{1,0:T(8,128)(2,1)}) %reduce-scatter.10.cloned.1.call-update) | async-done | bytes 688144 | tf_op jit(solution)/shard_map/reduce_scatter | solution.py:413
  503.8 49.7 %all-gather.13.cloned.1.call-done = bf16[4,224,1216]{2,1,0:T(8,128)(2,1)} async-done(((bf16[4,56,1216]{2,1,0:T(8,128)(2,1)}), bf16[4,224,1216]{2,1,0:T(8,128)(2,1)}) %all-gather.13.cloned.1.call-update) | async-done | bytes 2179088 | tf_op jit(solution)/shard_map/all_gather | solution.py:427
  553.5 6.5 reshape.300
  560.0 7.6 %copy.117 = f32[224,2,4,608]{3,2,1,0:T(4,128)} copy(f32[224,2,4,608]{3,1,0,2:T(2,128)} %bitcast.89) | data formatting | bytes 8716288 | tf_op jit(solution)/shard_map/convert_element_type | solution.py:432
  567.6 8.5 %reshape.297 = f32[224,2,2432]{2,1,0:T(2,128)} reshape(f32[224,2,4,608]{3,2,1,0:T(4,128)} %copy.117) | data formatting | bytes 8716288 | tf_op jit(solution)/shard_map/convert_element_type | solution.py:432
  576.1 54.0 %all-reduce.10.cloned.1.call-done = (bf16[4,608,224]{2,0,1:T(4,128)(2,1)}, bf16[240,1024]{1,0:T(8,128)(2,1)}) async-done(((bf16[4,608,224]{2,0,1:T(4,128)(2,1)}, bf16[240,1024]{1,0:T(8,128)(2,1)}), (bf16[4,608,224]{2,0,1:T(4,128)(2,1)}, bf16[240,1024]{1,0:T(8,128)(2,1)})) %all-reduce.10.cloned.1.call-update) | async-done | bytes 1581072
  631.9 4.1 all-to-all-start.3
  637.2 4.3 all-to-all-done.3
  641.6 1.8 copy.121
  643.4 3.2 fusion.19
  646.7 42.1 %psum.14 = f32[2,896]{1,0:T(2,128)S(1)} all-reduce(f32[2,896]{1,0:T(2,128)S(1)} %pad_maximum_fusion.10), channel_id=1, replica_groups=mesh['fsdp'=4,'ctx'=4,'tp'=2] {'fsdp','ctx'}, use_global_device_ids=true, to_apply=%region_13.14 | all-reduce | flops 1792 | bytes 14336 | tf_op jit(solution)/shard_map/psum | solution.py:482
  689.5 5.4 fusion.18
  697.5 2.7 copy.122
  700.8 2.2 reshape.298
  (165 shorter events, 33.5 us)
Async XLA Ops:
  7.2 5.0 copy-start.34
  7.2 5.0 copy-start.26
  7.2 22.4 %copy-start.6 = (bf16[768,896]{1,0:T(8,128)(2,1)S(1)}, bf16[768,896]{1,0:T(8,128)(2,1)}, u32[]{:S(2)}) copy-start(bf16[768,896]{1,0:T(8,128)(2,1)} %param.10) | copy-start | bytes 4128772
  7.2 37.1 %all-gather.17.cloned.1.call-start = ((), (), s32[]{:S(2)}) async-start(), calls=%async_computation.16 | async-start | bytes 1474560 | tf_op jit(solution)/shard_map/all_gather | solution.py:345
  12.1 157.6 %all-gather.9.cloned.1.call-start = ((), (), s32[]{:S(2)}) async-start(), calls=%async_computation.9 | async-start | bytes 6193152 | tf_op jit(solution)/shard_map/all_gather | solution.py:396
  29.6 59.6 %copy-start.12 = (bf16[448,896]{0,1:T(8,128)(2,1)}, bf16[448,896]{0,1:T(8,128)(2,1)S(1)}, u32[]{:S(2)}) copy-start(bf16[448,896]{0,1:T(8,128)(2,1)S(1)} %all_gather.31) | copy-start | bytes 2408452
  30.0 22.0 %copy-start.27 = (f32[768]{0:T(1024)}, f32[768]{0:T(1024)S(1)}, u32[]{:S(2)}) copy-start(f32[768]{0:T(1024)S(1)} %add_rsqrt_fusion.1) | copy-start | bytes 9220
  30.4 21.6 %copy-start.21 = (f32[32,768]{1,0:T(8,128)}, f32[32,768]{1,0:T(8,128)S(1)}, u32[]{:S(2)}) copy-start(f32[32,768]{1,0:T(8,128)S(1)} %get-tuple-element.109) | copy-start | bytes 294916
  30.4 21.6 %copy-start.22 = (f32[32,768]{1,0:T(8,128)}, f32[32,768]{1,0:T(8,128)S(1)}, u32[]{:S(2)}) copy-start(f32[32,768]{1,0:T(8,128)S(1)} %get-tuple-element.110) | copy-start | bytes 294916
  45.8 6.2 copy-start.30
  89.2 8.5 %copy-start.1 = (f32[8,768]{1,0:T(8,128)}, f32[8,768]{1,0:T(8,128)S(1)}, u32[]{:S(2)}) copy-start(f32[8,768]{1,0:T(8,128)S(1)} %get-tuple-element.14.log_ref) | copy-start | bytes 73732
  91.3 3.5 collective-permute-start
  91.4 6.3 copy-start.7
  100.0 1.5 copy-start.9
  101.5 1.6 copy-start.14
  102.5 113.7 %all-gather.11.cloned.1.call-start = ((), (), s32[]{:S(2)}) async-start(), calls=%async_computation.11 | async-start | bytes 6193152 | tf_op jit(solution)/shard_map/all_gather | solution.py:386
  122.1 44.0 %all-to-all-start = ((bf16[4,224,1216]{2,1,0:T(8,128)(2,1)}), bf16[4,224,1216]{2,1,0:T(8,128)(2,1)}, u32[]{:S(2)}, u32[]{:S(2)}) async-start(bf16[4,224,1216]{2,1,0:T(8,128)(2,1)} %reshape.286), calls=%async_computation | async-start | bytes 4587520 | tf_op jit(solution)/shard_map/all_to_all | solution.py:378
  166.1 24.9 %all-to-all-start.1 = ((bf16[4,608,224]{1,2,0:T(8,128)(2,1)}), bf16[4,608,224]{1,2,0:T(8,128)(2,1)S(1)}, u32[]{:S(2)}, u32[]{:S(2)}) async-start(bf16[4,608,224]{1,2,0:T(8,128)(2,1)} %copy.111), calls=%async_computation.1 | async-start | bytes 2293760 | tf_op jit(solution)/shard_map/all_to_all | solution.py:382
  169.6 132.0 %reduce-scatter.12.cloned.1.call-start = ((), (), s32[]{:S(2)}) async-start(), calls=%async_computation.12 | async-start | bytes 6193152 | tf_op jit(solution)/shard_map/reduce_scatter | solution.py:407
  191.0 37.9 %copy-start.19 = (bf16[4,608,224]{1,2,0:T(8,128)(2,1)}, bf16[4,608,224]{1,2,0:T(8,128)(2,1)S(1)}, u32[]{:S(2)}) copy-start(bf16[4,608,224]{1,2,0:T(8,128)(2,1)S(1)} %all-to-all-done.1) | copy-start | bytes 3268612
  228.9 1.9 copy-start.36
  228.9 3.0 copy-start.37
  243.7 117.0 %reduce-scatter.14.cloned.1.call-start = ((), (), s32[]{:S(2)}) async-start(), calls=%async_computation.13 | async-start | bytes 983040 | tf_op jit(solution)/shard_map/reduce_scatter | solution.py:453
  301.7 2.4 collective-permute-start.2
  301.7 3.6 copy-start.10
  305.3 1.3 copy-start.15
  306.6 1.2 copy-start.13
  307.8 21.6 %copy-start.3 = (f32[768,896]{1,0:T(8,128)}, f32[768,896]{1,0:T(8,128)S(1)}, u32[]{:S(2)}) copy-start(f32[768,896]{1,0:T(8,128)S(1)} %fusion.11) | copy-start | bytes 8257540
  307.8 0.9 copy-start.2
  329.4 0.9 copy-start
  330.3 72.7 %reduce-scatter.16.cloned.1.call-start = ((), (), s32[]{:S(2)}) async-start(), calls=%async_computation.17 | async-start | bytes 2723840
  357.5 83.4 %reduce-scatter.18.cloned.1.call-start = ((), (), s32[]{:S(2)}) async-start(), calls=%async_computation.18 | async-start | bytes 2457600
  357.5 2.3 copy-start.4
  359.8 8.9 %copy-start.11 = (f32[448,768]{1,0:T(8,128)S(1)}, f32[448,768]{1,0:T(8,128)}, u32[]{:S(2)}) copy-start(f32[448,768]{1,0:T(8,128)} %broadcast_multiply_fusion.1) | copy-start | bytes 4128772
  361.7 0.7 copy-start.16
  363.2 8.8 %copy-start.8 = (bf16[768,896]{1,0:T(8,128)(2,1)S(1)}, bf16[768,896]{1,0:T(8,128)(2,1)}, u32[]{:S(2)}) copy-start(bf16[768,896]{1,0:T(8,128)(2,1)} %param.10) | copy-start | bytes 4128772
  368.7 3.3 copy-start.28
  368.7 3.3 copy-start.31
  371.1 0.9 copy-start.23
  377.6 1.7 copy-start.20
  379.1 123.4 %reduce-scatter.10.cloned.1.call-start = ((), (), s32[]{:S(2)}) async-start(), calls=%async_computation.10 | async-start | bytes 6193152 | tf_op jit(solution)/shard_map/reduce_scatter | solution.py:413
  388.3 165.2 %all-gather.13.cloned.1.call-start = ((), (), s32[]{:S(2)}) async-start(), calls=%async_computation.14 | async-start | bytes 2867200 | tf_op jit(solution)/shard_map/all_gather | solution.py:427
  421.0 209.1 %all-reduce.10.cloned.1.call-start = ((), (), s32[]{:S(2)}) async-start(), calls=%async_computation.19 | async-start | bytes 3473408
  429.0 11.9 %copy-start.18 = (bf16[4,224,576]{2,1,0:T(8,128)(2,1)S(1)}, bf16[4,224,576]{2,1,0:T(8,128)(2,1)}, u32[]{:S(2)}) copy-start(bf16[4,224,576]{2,1,0:T(8,128)(2,1)} %copy.108) | copy-start | bytes 3096580
  430.1 10.8 %copy-start.24 = (bf16[9,64,768]{2,1,0:T(8,128)(2,1)S(1)}, bf16[9,64,768]{2,1,0:T(8,128)(2,1)}, u32[]{:S(2)}) copy-start(bf16[9,64,768]{2,1,0:T(8,128)(2,1)} %copy-done.23) | copy-start | bytes 2654212
  440.9 61.7 %copy-start.35 = (u32[32]{0:T(128)S(1)}, u32[32]{0:T(128)}, u32[]{:S(2)}) copy-start(u32[32]{0:T(128)} %constant.79) | copy-start | bytes 388
  443.4 200.0 %collective-permute-start.3 = (bf16[768,896]{1,0:T(8,128)(2,1)}, bf16[768,896]{1,0:T(8,128)(2,1)}, u32[]{:S(2)}, u32[]{:S(2)}) collective-permute-start(bf16[768,896]{1,0:T(8,128)(2,1)} %convolution_convert_fusion.2), channel_id=1, source_target_pairs={{0,1},{1,0},{2,3},{3,2},{4,5},{5,4},{6,7},{7,6},{8,9},{9,8},{10,11... | collective-permute-start | bytes 4128776 | tf_op jit(solution)/shard_map/ppermute | solution.py:292
  502.5 133.7 %collective-permute-start.1 = (bf16[384,896]{1,0:T(8,128)(2,1)}, bf16[384,896]{1,0:T(8,128)(2,1)S(1)}, u32[]{:S(2)}, u32[]{:S(2)}) collective-permute-start(bf16[384,896]{1,0:T(8,128)(2,1)} %reduce-scatter.10.cloned.1.call-done), channel_id=1, source_target_pairs={{0,1},{1,0},{2,3},{3,2},{4,5},{5,4},{6,7},{7,6},{8,9},{9,8},{10,11... | collective-permute-start | bytes 2064392 | tf_op jit(solution)/shard_map/ppermute | solution.py:299
  567.6 8.5 %copy-start.33 = (f32[896]{0:T(1024)S(1)}, f32[896]{0:T(1024)}, u32[]{:S(2)}) copy-start(f32[896]{0:T(1024)} %get-tuple-element.82) | copy-start | bytes 10756
  567.6 68.6 %copy-start.25 = (bf16[384,896]{1,0:T(8,128)(2,1)S(1)}, bf16[384,896]{1,0:T(8,128)(2,1)}, u32[]{:S(2)}) copy-start(bf16[384,896]{1,0:T(8,128)(2,1)} %reduce-scatter.10.cloned.1.call-done) | copy-start | bytes 2064388
  630.1 13.3 %copy-start.29 = (f32[768]{0:T(1024)S(1)}, f32[768]{0:T(1024)}, u32[]{:S(2)}) copy-start(f32[768]{0:T(1024)} %copy-done.27) | copy-start | bytes 9220
  630.1 13.4 %copy-start.32 = (f32[896]{0:T(1024)S(1)}, f32[896]{0:T(1024)}, u32[]{:S(2)}) copy-start(f32[896]{0:T(1024)} %copy-done.30) | copy-start | bytes 10756
  631.9 9.7 %all-to-all-start.3 = ((bf16[4,152,224]{2,1,0:T(8,128)(2,1)}), bf16[4,152,224]{2,1,0:T(8,128)(2,1)}, u32[]{:S(2)}, u32[]{:S(2)}) async-start(bf16[4,152,224]{2,1,0:T(8,128)(2,1)} %copy.120), calls=%async_computation.6 | async-start | bytes 622592 | tf_op jit(solution)/shard_map/all_to_all | solution.py:440
  636.0 61.5 %all-gather.15.cloned.1.call-start = ((), (), s32[]{:S(2)}) async-start(), calls=%async_computation.15 | async-start | bytes 1556480 | tf_op jit(solution)/shard_map/all_gather | solution.py:441
  637.2 52.2 %copy-start.5 = (f32[768,896]{1,0:T(8,128)S(1)}, f32[768,896]{1,0:T(8,128)}, u32[]{:S(2)}) copy-start(f32[768,896]{1,0:T(8,128)} %copy-done.3) | copy-start | bytes 8257540
  689.5 5.4 copy-start.17
Sparse Core Ops, SparseCore 0:
  12.2 32.0 all-gather.16
  102.6 64.5 all-gather.8
  169.1 47.0 all-gather.10
  243.8 57.8 reduce-scatter.11
  330.4 23.2 reduce-scatter.13
  357.6 45.3 reduce-scatter.15
  406.4 34.4 reduce-scatter.17
  444.7 57.8 reduce-scatter.9
  504.1 49.3 all-gather.12
  556.4 73.6 all-reduce.9
  643.5 32.4 all-gather.14
